TPU v7x, 32 devices: a whole 2x2x4 slice. The times are simulated.
32 devices in a mesh: parts: 2 (over x), gy: 16 (over z, y, core).
Axes of the slice: x: 2, y: 2, z: 4, core: 2. Of those that a mesh axis runs over, the one named last changes fastest.
Arguments:
- measured: bfloat16 [8, 32, 256, 128], P(None, None, ('parts', 'gy')), parts along dimension 2, may hold values from 0.19921875 to 8
- start: float32 [32, 256, 128], P(None, ('parts', 'gy')), parts along dimension 1, may hold values from 0.5 to 4
- psf: float32 [8, 15, 7, 7], replicated, may hold values from 0.05 to 1
- background: float32 [8], replicated, may hold values from 0.2 to 2
Outputs:
- estimate: float32 [32, 256, 128], P(None, ('parts', 'gy')), parts along dimension 1
There are 2 independent parts, one for each index of `parts`. A program takes and returns all parts, laid end to end along the dimension named above; an argument that names none is the same for every part. Nothing has to cross between parts.
All inputs are finite; a program needn't handle non-finite values.
Results may differ from a plain program's by a relative error of at most 0.0003.
Values may be sent and summed in bfloat16 or wider, within the bound.
A program may use at most 128 MiB of HBM per device.

v0:
```python
import functools

import jax
import jax.numpy as jnp
from jax import lax
from jax.experimental import pallas as pl
from jax.experimental.pallas import tpu as pltpu
from jax.sharding import PartitionSpec as P

F32 = jnp.float32
BF16 = jnp.bfloat16


def shift_cols(x, by):
    cols = x.shape[1]
    if by == 0:
        return x
    lane = lax.broadcasted_iota(jnp.int32, x.shape, 1)
    rolled = pltpu.roll(x, (-by) % cols, 1)
    keep = lane < cols - by if by > 0 else lane >= -by
    return jnp.where(keep, rolled, 0.0)


def kernel(
    dims, measured, start, psf, background, out,
    taps, corr_w, blur_w, rows_pad, shifted, recorded, ratio, sent, got,
    send_sem, recv_sem,
):
    views, depth, ky, kx, planes, rows, cols, size = dims
    hz, hy, hx = depth // 2, ky // 2, kx // 2
    wide = views * planes
    me = lax.axis_index("gy")
    has_prev = me > 0
    has_next = me < size - 1
    prev = {"gy": jnp.maximum(me - 1, 0)}
    nxt = {"gy": jnp.minimum(me + 1, size - 1)}

    barrier = pltpu.get_barrier_semaphore()

    @pl.when(has_prev)
    def _():
        pl.semaphore_signal(barrier, inc=1, device_id=prev, device_id_type=pl.DeviceIdType.MESH)

    @pl.when(has_next)
    def _():
        pl.semaphore_signal(barrier, inc=1, device_id=nxt, device_id_type=pl.DeviceIdType.MESH)

    for y in range(rows):
        rows_pad[hy + y] = start[:, y, :].astype(BF16)

    def halo(to_prev):
        if to_prev:
            src, dst = rows_pad.at[pl.ds(hy, hy)], rows_pad.at[pl.ds(hy + rows, hy)]
        else:
            src, dst = rows_pad.at[pl.ds(rows, hy)], rows_pad.at[pl.ds(0, hy)]
        i = 0 if to_prev else 1
        return pltpu.make_async_remote_copy(
            src_ref=src, dst_ref=dst, send_sem=send_sem.at[i], recv_sem=recv_sem.at[i],
            device_id=prev if to_prev else nxt, device_id_type=pl.DeviceIdType.MESH,
        )

    def partial(to_prev):
        i = 0 if to_prev else 1
        return pltpu.make_async_remote_copy(
            src_ref=sent.at[i], dst_ref=got.at[i], send_sem=send_sem.at[2 + i], recv_sem=recv_sem.at[2 + i],
            device_id=prev if to_prev else nxt, device_id_type=pl.DeviceIdType.MESH,
        )

    pl.semaphore_wait(barrier, (me + size - 1) // size + (2 * size - 2 - me) // size)

    @pl.when(has_prev)
    def _():
        halo(True).start()

    @pl.when(has_next)
    def _():
        halo(False).start()

    total = jnp.sum(jnp.sum(psf[...], axis=(0, 1)), axis=1, keepdims=True)
    taps[:, :, :depth] = (psf[...] / total).astype(BF16).astype(F32).reshape(ky * kx, views, depth)
    per_tile = 128 // planes
    lane = lax.broadcasted_iota(jnp.int32, (ky * kx, 128), 1)
    tiles = []
    for first in range(0, views, per_tile):
        tile = jnp.zeros((ky * kx, 128), F32)
        for j in range(per_tile):
            part = taps[:, first + j, :]
            if j:
                part = pltpu.roll(part, j * planes, 1)
            tile = jnp.where((lane >= j * planes) & (lane < j * planes + depth), part, tile)
        tiles.append(tile)
    flat = jnp.concatenate(tiles, axis=1)
    corr_w[kx * planes :] = jnp.zeros((wide - kx * planes, ky * wide), BF16)
    q_of = lax.broadcasted_iota(jnp.int32, (planes, wide), 0)
    p_of = lax.broadcasted_iota(jnp.int32, (planes, wide), 1) % planes
    band = jnp.abs(p_of - q_of) <= hz
    eye = (
        lax.broadcasted_iota(jnp.int32, (wide, wide), 0)
        == lax.broadcasted_iota(jnp.int32, (wide, wide), 1)
    ).astype(BF16)
    for b in range(ky):
        for c in range(kx):
            i = b * kx + c
            line = jnp.broadcast_to(flat[i : i + 1], (planes, wide))
            line = pltpu.roll(line, wide - hz, 1, stride=1, stride_axis=0)
            corr_w[c * planes : (c + 1) * planes, b * wide : (b + 1) * wide] = jnp.where(band, line, 0.0).astype(BF16)
        blur_w[:, b * wide : (b + 1) * wide] = lax.dot_general(
            eye, corr_w[:, b * wide : (b + 1) * wide], (((1,), (1,)), ((), ())), preferred_element_type=F32
        ).astype(BF16)

    recorded[...] = measured[...].astype(F32)
    ratio[:, :cols] = jnp.zeros((wide, cols), BF16)
    ratio[:, (rows + 1) * cols :] = jnp.zeros((wide, cols), BF16)
    shifted[kx * planes :] = jnp.zeros((wide - kx * planes, (rows + 2 * hy) * cols), BF16)

    def spread(y):
        line = rows_pad[y].astype(F32)
        for c in range(kx):
            shifted[c * planes : (c + 1) * planes, y * cols : (y + 1) * cols] = shift_cols(line, hx - c).astype(BF16)

    for y in range(hy, hy + rows):
        spread(y)

    @pl.when(has_prev)
    def _():
        halo(True).wait_send()
        halo(False).wait_recv()

    @pl.when(jnp.logical_not(has_prev))
    def _():
        rows_pad[:hy] = jnp.zeros((hy, planes, cols), BF16)

    @pl.when(has_next)
    def _():
        halo(False).wait_send()
        halo(True).wait_recv()

    @pl.when(jnp.logical_not(has_next))
    def _():
        rows_pad[hy + rows :] = jnp.zeros((hy, planes, cols), BF16)

    for y in range(hy):
        spread(y)
        spread(hy + rows + y)

    offsets = jnp.concatenate([jnp.full((planes, cols), background[v], F32) for v in range(views)], axis=0)
    for t in range(rows // 2):
        operand = jnp.concatenate(
            [shifted[:, (2 * t + ky - 1 - b) * cols : (2 * t + ky + 1 - b) * cols] for b in range(ky)], axis=0
        )
        blurred = jnp.dot(blur_w[...], operand, preferred_element_type=F32)
        for j in range(2):
            y = 2 * t + j
            below = blurred[:, j * cols : (j + 1) * cols] + offsets
            ratio[:, (y + 1) * cols : (y + 2) * cols] = (recorded[:, y, :] / below).astype(BF16)

    def correlate(r):
        used = [b for b in range(ky) if -1 <= r + b - hy <= rows - 1]
        weights = jnp.concatenate([corr_w[: kx * planes, b * wide : (b + 1) * wide] for b in used], axis=1)
        operand = jnp.concatenate(
            [ratio[:, (r + b - hy + 1) * cols : (r + b - hy + 3) * cols] for b in used], axis=0
        )
        every = jnp.dot(weights, operand, preferred_element_type=F32)
        results = []
        for j in range(2):
            total = jnp.zeros((planes, cols), F32)
            for c in range(kx):
                total += shift_cols(every[c * planes : (c + 1) * planes, j * cols : (j + 1) * cols], c - hx)
            results.append(total)
        return results

    _, sent[0, 0] = correlate(-4)
    sent[0, 1], sent[0, 2] = correlate(-2)

    @pl.when(has_prev)
    def _():
        partial(True).start()

    sent[1, 0], sent[1, 1] = correlate(rows)
    sent[1, 2], _ = correlate(rows + 2)

    @pl.when(has_next)
    def _():
        partial(False).start()

    for t in range(rows // 2):
        out[:, 2 * t, :], out[:, 2 * t + 1, :] = correlate(2 * t)

    @pl.when(has_prev)
    def _():
        partial(False).wait_recv()
        for y in range(hy):
            out[:, y, :] += got[1, y]
        partial(True).wait_send()

    @pl.when(has_next)
    def _():
        partial(True).wait_recv()
        for y in range(hy):
            out[:, rows - hy + y, :] += got[0, y]
        partial(False).wait_send()


def local(size, measured, start, psf, background):
    views, planes, rows, cols = measured.shape
    _, depth, ky, kx = psf.shape
    hy = ky // 2
    wide = views * planes
    dims = (views, depth, ky, kx, planes, rows, cols, size)
    total = pl.pallas_call(
        functools.partial(kernel, dims),
        out_shape=jax.ShapeDtypeStruct((planes, rows, cols), F32),
        in_specs=[pl.BlockSpec(memory_space=pltpu.VMEM)] * 3 + [pl.BlockSpec(memory_space=pltpu.SMEM)],
        out_specs=pl.BlockSpec(memory_space=pltpu.VMEM),
        scratch_shapes=[
            pltpu.VMEM((ky * kx, views, 128), F32),
            pltpu.VMEM((wide, ky * wide), BF16),
            pltpu.VMEM((wide, ky * wide), BF16),
            pltpu.VMEM((rows + 2 * hy, planes, cols), BF16),
            pltpu.VMEM((wide, (rows + 2 * hy) * cols), BF16),
            pltpu.VMEM((wide, rows, cols), F32),
            pltpu.VMEM((wide, (rows + 2) * cols), BF16),
            pltpu.VMEM((2, hy, planes, cols), F32),
            pltpu.VMEM((2, hy, planes, cols), F32),
            pltpu.SemaphoreType.DMA((4,)),
            pltpu.SemaphoreType.DMA((4,)),
        ],
        compiler_params=pltpu.CompilerParams(
            collective_id=0, has_side_effects=True, vmem_limit_bytes=48 * 1024 * 1024
        ),
    )(measured.reshape(wide, rows, cols), start, jnp.transpose(psf, (2, 3, 0, 1)), background)
    return start * total / views


def solution(mesh):
    in_specs = (P(None, None, ("parts", "gy"), None), P(None, ("parts", "gy"), None), P(), P())
    out_specs = P(None, ("parts", "gy"), None)
    body = functools.partial(local, mesh.shape["gy"])
    return jax.shard_map(body, mesh=mesh, in_specs=in_specs, out_specs=out_specs, check_vma=False)
```

profile of v0, /device:TPU:5, one launch (start us, length us, event | category | flops | bytes accessed | tf_op | source)
XLA Modules:
  0.0 14.6 jit_solution(17644594365640510544)
XLA Ops:
  0.0 0.0 copy-start.3
  0.0 0.7 %copy-done.3 = f32[8]{0:T(128)S(1)} copy-done((f32[8]{0:T(128)S(1)}, f32[8]{0:T(128)}, u32[]{:S(2)}) %copy-start.3) | copy-done | bytes 56
  0.7 0.0 copy-start
  0.7 0.9 %copy-done = f32[32,8,128]{2,1,0:T(8,128)S(1)} copy-done((f32[32,8,128]{2,1,0:T(8,128)S(1)}, f32[32,8,128]{2,1,0:T(8,128)}, u32[]{:S(2)}) %copy-start) | copy-done | bytes 131096
  1.6 0.0 copy-start.1
  1.6 1.0 %copy-done.1 = bf16[8,32,8,128]{3,2,1,0:T(8,128)(2,1)S(1)} copy-done((bf16[8,32,8,128]{3,2,1,0:T(8,128)(2,1)S(1)}, bf16[8,32,8,128]{3,2,1,0:T(8,128)(2,1)}, u32[]{:S(2)}) %copy-start.1) | copy-done | bytes 524312
  2.6 0.0 copy-start.2
  2.6 0.9 %copy-done.2 = f32[8,15,7,7]{1,0,3,2:T(8,128)S(1)} copy-done((f32[8,15,7,7]{1,0,3,2:T(8,128)S(1)}, f32[8,15,7,7]{1,0,3,2:T(8,128)}, u32[]{:S(2)}) %copy-start.2) | copy-done | bytes 23544
  3.5 10.4 %shard_map.46 = f32[32,8,128]{2,1,0:T(8,128)S(1)} custom-call(bf16[256,8,128]{2,1,0:T(8,128)(2,1)S(1)} %bitcast.2, f32[32,8,128]{2,1,0:T(8,128)S(1)} %copy-done, f32[7,7,8,15]{3,2,1,0:T(8,128)S(1)} %bitcast.3, f32[8]{0:T(128)S(1)} %copy-done.3), custom_call_target="tpu_custom_call" | custom-call | tf_op jit(solution)/shard_map/pallas_call | solution.py:210
  14.0 0.7 %multiply_multiply_fusion = f32[32,8,128]{2,1,0:T(8,128)} fusion(f32[32,8,128]{2,1,0:T(8,128)S(1)} %copy-done, f32[32,8,128]{2,1,0:T(8,128)S(1)} %shard_map.46), kind=kLoop, calls=%fused_computation | loop fusion | flops 65536 | bytes 393216 | tf_op jit(solution)/shard_map/div | solution.py:232
Async XLA Ops:
  0.0 0.7 %copy-start.3 = (f32[8]{0:T(128)S(1)}, f32[8]{0:T(128)}, u32[]{:S(2)}) copy-start(f32[8]{0:T(128)} %background.1) | copy-start | bytes 100
  0.7 0.9 %copy-start = (f32[32,8,128]{2,1,0:T(8,128)S(1)}, f32[32,8,128]{2,1,0:T(8,128)}, u32[]{:S(2)}) copy-start(f32[32,8,128]{2,1,0:T(8,128)} %start.1) | copy-start | bytes 393220
  1.6 1.0 %copy-start.1 = (bf16[8,32,8,128]{3,2,1,0:T(8,128)(2,1)S(1)}, bf16[8,32,8,128]{3,2,1,0:T(8,128)(2,1)}, u32[]{:S(2)}) copy-start(bf16[8,32,8,128]{3,2,1,0:T(8,128)(2,1)} %param.4) | copy-start | bytes 1572868
  2.6 0.9 %copy-start.2 = (f32[8,15,7,7]{1,0,3,2:T(8,128)S(1)}, f32[8,15,7,7]{1,0,3,2:T(8,128)}, u32[]{:S(2)}) copy-start(f32[8,15,7,7]{1,0,3,2:T(8,128)} %param.6) | copy-start | bytes 70564
where the time goes:
time: 14.9 us; the launch traced here: 14.6 us
  Pallas kernels  10.4 us (70%)
  local copies, waits for them, and re-layouts  3.53 us (24%)
  other arithmetic  0.68 us (5%)
    pallas_call x1, Pallas kernels, local(): pl.pallas_call(functools.partial(kernel, dims), out_shape=jax.ShapeDtypeS...  10.4 us
    unnamed x8, local copies, waits for them, and re-layouts  3.53 us
    div x1, other arithmetic, local(): return start * total / views  0.68 us

commit v1 on v0

--- a/solution.py
+++ b/solution.py
@@ -22,9 +22,9 @@
 
 
 def kernel(
-    dims, measured, start, psf, background, out,
-    taps, corr_w, blur_w, rows_pad, shifted, recorded, ratio, sent, got,
-    send_sem, recv_sem,
+    dims, measured_hbm, start_hbm, psf_hbm, background_hbm, out,
+    measured, start, psf, background, taps, corr_w, blur_w, rows_pad, shifted, recorded, ratio, sent, got,
+    send_sem, recv_sem, load_sem,
 ):
     views, depth, ky, kx, planes, rows, cols, size = dims
     hz, hy, hx = depth // 2, ky // 2, kx // 2
@@ -35,6 +35,15 @@
     prev = {"gy": jnp.maximum(me - 1, 0)}
     nxt = {"gy": jnp.minimum(me + 1, size - 1)}
 
+    loads = [
+        pltpu.make_async_copy(src, dst, load_sem.at[i])
+        for i, (src, dst) in enumerate(
+            [(start_hbm, start), (psf_hbm, psf), (measured_hbm, measured), (background_hbm, background)]
+        )
+    ]
+    loads[0].start()
+    loads[1].start()
+
     barrier = pltpu.get_barrier_semaphore()
 
     @pl.when(has_prev)
@@ -45,6 +54,9 @@
     def _():
         pl.semaphore_signal(barrier, inc=1, device_id=nxt, device_id_type=pl.DeviceIdType.MESH)
 
+    loads[0].wait()
+    loads[2].start()
+    loads[3].start()
     for y in range(rows):
         rows_pad[hy + y] = start[:, y, :].astype(BF16)
 
@@ -76,6 +88,7 @@
     def _():
         halo(False).start()
 
+    loads[1].wait()
     total = jnp.sum(jnp.sum(psf[...], axis=(0, 1)), axis=1, keepdims=True)
     taps[:, :, :depth] = (psf[...] / total).astype(BF16).astype(F32).reshape(ky * kx, views, depth)
     per_tile = 128 // planes
@@ -108,6 +121,8 @@
             eye, corr_w[:, b * wide : (b + 1) * wide], (((1,), (1,)), ((), ())), preferred_element_type=F32
         ).astype(BF16)
 
+    loads[2].wait()
+    loads[3].wait()
     recorded[...] = measured[...].astype(F32)
     ratio[:, :cols] = jnp.zeros((wide, cols), BF16)
     ratio[:, (rows + 1) * cols :] = jnp.zeros((wide, cols), BF16)
@@ -121,30 +136,9 @@
     for y in range(hy, hy + rows):
         spread(y)
 
-    @pl.when(has_prev)
-    def _():
-        halo(True).wait_send()
-        halo(False).wait_recv()
-
-    @pl.when(jnp.logical_not(has_prev))
-    def _():
-        rows_pad[:hy] = jnp.zeros((hy, planes, cols), BF16)
-
-    @pl.when(has_next)
-    def _():
-        halo(False).wait_send()
-        halo(True).wait_recv()
-
-    @pl.when(jnp.logical_not(has_next))
-    def _():
-        rows_pad[hy + rows :] = jnp.zeros((hy, planes, cols), BF16)
-
-    for y in range(hy):
-        spread(y)
-        spread(hy + rows + y)
-
     offsets = jnp.concatenate([jnp.full((planes, cols), background[v], F32) for v in range(views)], axis=0)
-    for t in range(rows // 2):
+
+    def blur(t):
         operand = jnp.concatenate(
             [shifted[:, (2 * t + ky - 1 - b) * cols : (2 * t + ky + 1 - b) * cols] for b in range(ky)], axis=0
         )
@@ -169,6 +163,18 @@
             results.append(total)
         return results
 
+    @pl.when(has_prev)
+    def _():
+        halo(False).wait_recv()
+
+    @pl.when(jnp.logical_not(has_prev))
+    def _():
+        rows_pad[:hy] = jnp.zeros((hy, planes, cols), BF16)
+
+    for y in range(hy):
+        spread(y)
+    for t in range((hy + 1) // 2):
+        blur(t)
     _, sent[0, 0] = correlate(-4)
     sent[0, 1], sent[0, 2] = correlate(-2)
 
@@ -176,6 +182,18 @@
     def _():
         partial(True).start()
 
+    @pl.when(has_next)
+    def _():
+        halo(True).wait_recv()
+
+    @pl.when(jnp.logical_not(has_next))
+    def _():
+        rows_pad[hy + rows :] = jnp.zeros((hy, planes, cols), BF16)
+
+    for y in range(hy):
+        spread(hy + rows + y)
+    for t in range(rows // 2 - 1, (hy + 1) // 2 - 1, -1):
+        blur(t)
     sent[1, 0], sent[1, 1] = correlate(rows)
     sent[1, 2], _ = correlate(rows + 2)
 
@@ -192,6 +210,7 @@
         for y in range(hy):
             out[:, y, :] += got[1, y]
         partial(True).wait_send()
+        halo(True).wait_send()
 
     @pl.when(has_next)
     def _():
@@ -199,6 +218,7 @@
         for y in range(hy):
             out[:, rows - hy + y, :] += got[0, y]
         partial(False).wait_send()
+        halo(False).wait_send()
 
 
 def local(size, measured, start, psf, background):
@@ -210,9 +230,13 @@
     total = pl.pallas_call(
         functools.partial(kernel, dims),
         out_shape=jax.ShapeDtypeStruct((planes, rows, cols), F32),
-        in_specs=[pl.BlockSpec(memory_space=pltpu.VMEM)] * 3 + [pl.BlockSpec(memory_space=pltpu.SMEM)],
+        in_specs=[pl.BlockSpec(memory_space=pltpu.HBM)] * 4,
         out_specs=pl.BlockSpec(memory_space=pltpu.VMEM),
         scratch_shapes=[
+            pltpu.VMEM((wide, rows, cols), BF16),
+            pltpu.VMEM((planes, rows, cols), F32),
+            pltpu.VMEM((ky, kx, views, depth), F32),
+            pltpu.SMEM((views,), F32),
             pltpu.VMEM((ky * kx, views, 128), F32),
             pltpu.VMEM((wide, ky * wide), BF16),
             pltpu.VMEM((wide, ky * wide), BF16),
@@ -224,9 +248,10 @@
             pltpu.VMEM((2, hy, planes, cols), F32),
             pltpu.SemaphoreType.DMA((4,)),
             pltpu.SemaphoreType.DMA((4,)),
+            pltpu.SemaphoreType.DMA((4,)),
         ],
         compiler_params=pltpu.CompilerParams(
-            collective_id=0, has_side_effects=True, vmem_limit_bytes=48 * 1024 * 1024
+            collective_id=0, has_side_effects=True, vmem_limit_bytes=63 * 1024 * 1024
         ),
     )(measured.reshape(wide, rows, cols), start, jnp.transpose(psf, (2, 3, 0, 1)), background)
     return start * total / views

time: 14.9 us -> 11.7 us (0.79)
  local copies, waits for them, and re-layouts: 3.53 us -> 0.01 us
  other arithmetic: 0.68 us -> 1.58 us
  Pallas kernels: 10.4 us -> 9.93 us
    unnamed x8 -> x2, local copies, waits for them, and re-layouts: 3.53 us -> 0.01 us
    div x1, other arithmetic: 0.68 us -> 1.58 us  [local(): return start * total / views]
    pallas_call x1, Pallas kernels: 10.4 us -> 9.93 us  [local(): pl.pallas_call(functools.partial(kernel, dims), out_shape=jax.ShapeDtypeS...]
where the time goes in v1:
time: 11.7 us; the launch traced here: 11.5 us
  Pallas kernels  9.93 us (85%)
  other arithmetic  1.58 us (14%)
    pallas_call x1, Pallas kernels, local(): pl.pallas_call(functools.partial(kernel, dims), out_shape=jax.ShapeDtypeS...  9.93 us
    div x1, other arithmetic, local(): return start * total / views  1.58 us

profile of v1, /device:TPU:5, one launch (start us, length us, event | category | flops | bytes accessed | tf_op | source)
XLA Modules:
  0.0 11.5 jit_solution(2386593290948207359)
XLA Ops:
  0.0 0.0 copy-start
  0.0 9.9 %shard_map.46 = f32[32,8,128]{2,1,0:T(8,128)} custom-call(bf16[256,8,128]{2,1,0:T(8,128)(2,1)} %bitcast.2, f32[32,8,128]{2,1,0:T(8,128)} %start_hbm.1, f32[7,7,8,15]{3,2,1,0:T(8,128)} %bitcast.3, f32[8]{0:T(128)} %background_hbm.1), custom_call_target="tpu_custom_call" | custom-call | tf_op jit(solution)/shard_map/pallas_call | solution.py:230
  9.9 0.0 copy-done
  9.9 1.6 %multiply_multiply_fusion = f32[32,8,128]{2,1,0:T(8,128)} fusion(f32[32,8,128]{2,1,0:T(8,128)S(1)} %copy-done, f32[32,8,128]{2,1,0:T(8,128)} %shard_map.46), kind=kLoop, calls=%fused_computation | loop fusion | flops 65536 | bytes 393216 | tf_op jit(solution)/shard_map/div | solution.py:257
Async XLA Ops:
  0.0 9.9 %copy-start = (f32[32,8,128]{2,1,0:T(8,128)S(1)}, f32[32,8,128]{2,1,0:T(8,128)}, u32[]{:S(2)}) copy-start(f32[32,8,128]{2,1,0:T(8,128)} %start_hbm.1) | copy-start | bytes 393220

commit v2 on v1

--- a/solution.py
+++ b/solution.py
@@ -107,19 +107,13 @@
     q_of = lax.broadcasted_iota(jnp.int32, (planes, wide), 0)
     p_of = lax.broadcasted_iota(jnp.int32, (planes, wide), 1) % planes
     band = jnp.abs(p_of - q_of) <= hz
-    eye = (
-        lax.broadcasted_iota(jnp.int32, (wide, wide), 0)
-        == lax.broadcasted_iota(jnp.int32, (wide, wide), 1)
-    ).astype(BF16)
     for b in range(ky):
         for c in range(kx):
             i = b * kx + c
             line = jnp.broadcast_to(flat[i : i + 1], (planes, wide))
             line = pltpu.roll(line, wide - hz, 1, stride=1, stride_axis=0)
             corr_w[c * planes : (c + 1) * planes, b * wide : (b + 1) * wide] = jnp.where(band, line, 0.0).astype(BF16)
-        blur_w[:, b * wide : (b + 1) * wide] = lax.dot_general(
-            eye, corr_w[:, b * wide : (b + 1) * wide], (((1,), (1,)), ((), ())), preferred_element_type=F32
-        ).astype(BF16)
+        blur_w[:, b * wide : (b + 1) * wide] = corr_w[:, b * wide : (b + 1) * wide].T
 
     loads[2].wait()
     loads[3].wait()
@@ -229,7 +223,7 @@
     dims = (views, depth, ky, kx, planes, rows, cols, size)
     total = pl.pallas_call(
         functools.partial(kernel, dims),
-        out_shape=jax.ShapeDtypeStruct((planes, rows, cols), F32),
+        out_shape=pltpu.VMEM((planes, rows, cols), F32),
         in_specs=[pl.BlockSpec(memory_space=pltpu.HBM)] * 4,
         out_specs=pl.BlockSpec(memory_space=pltpu.VMEM),
         scratch_shapes=[

time: 11.7 us -> 9.94 us (0.85)
  other arithmetic: 1.58 us -> 0.67 us
  Pallas kernels: 9.93 us -> 9.1 us
    div x1, other arithmetic: 1.58 us -> 0.67 us  [local(): return start * total / views]
    pallas_call x1, Pallas kernels: 9.93 us -> 9.1 us  [local(): pl.pallas_call(functools.partial(kernel, dims), out_shape=pltpu.VMEM((pla...]
where the time goes in v2:
time: 9.94 us; the launch traced here: 9.8 us
  Pallas kernels  9.1 us (92%)
  other arithmetic  0.67 us (7%)
    pallas_call x1, Pallas kernels, local(): pl.pallas_call(functools.partial(kernel, dims), out_shape=pltpu.VMEM((pla...  9.1 us
    div x1, other arithmetic, local(): return start * total / views  0.67 us

profile of v2, /device:TPU:5, one launch (start us, length us, event | category | flops | bytes accessed | tf_op | source)
XLA Modules:
  0.0 9.8 jit_solution(18195586332260145555)
XLA Ops:
  0.0 0.0 copy-start
  0.0 9.1 %shard_map.46 = f32[32,8,128]{2,1,0:T(8,128)S(1)} custom-call(bf16[256,8,128]{2,1,0:T(8,128)(2,1)} %bitcast.2, f32[32,8,128]{2,1,0:T(8,128)} %start_hbm.1, f32[7,7,8,15]{3,2,1,0:T(8,128)} %bitcast.3, f32[8]{0:T(128)} %background_hbm.1), custom_call_target="tpu_custom_call" | custom-call | tf_op jit(solution)/shard_map/pallas_call | solution.py:224
  9.1 0.0 copy-done
  9.1 0.7 %multiply_multiply_fusion = f32[32,8,128]{2,1,0:T(8,128)} fusion(f32[32,8,128]{2,1,0:T(8,128)S(1)} %copy-done, f32[32,8,128]{2,1,0:T(8,128)S(1)} %shard_map.46), kind=kLoop, calls=%fused_computation | loop fusion | flops 65536 | bytes 393216 | tf_op jit(solution)/shard_map/div | solution.py:251
Async XLA Ops:
  0.0 9.1 %copy-start = (f32[32,8,128]{2,1,0:T(8,128)S(1)}, f32[32,8,128]{2,1,0:T(8,128)}, u32[]{:S(2)}) copy-start(f32[32,8,128]{2,1,0:T(8,128)} %start_hbm.1) | copy-start | bytes 393220
